TPU v7x, 128 devices: a whole 4x4x4 slice. The times are simulated.
128 devices in a mesh: tp: 16 (over y, z_lo, core), dp: 8 (over x, z_hi).
Axes of the slice: x: 4, y: 4, z: 4 (z_hi: 2, z_lo: 2; z = z_hi * 2 + z_lo), core: 2. Of those that a mesh axis runs over, the one named last changes fastest.
Arguments:
- tokens: bfloat16 [16, 1024, 2048], P('dp', 'tp'), may hold values from -6 to 6
- lengths: int32 [16], P('dp'), may hold values from 150 to 1024, as said below
- exit_layers: int32 [16, 1024], P('dp'), may hold values from 1 to 24
- weight_query: bfloat16 [2048, 2048], P(None, 'tp'), may hold values from -0.125 to 0.125
- bias_query: float32 [2048], P('tp'), may hold values from -3 to 3
- weight_key: bfloat16 [2048, 2048], P(None, 'tp'), may hold values from -0.125 to 0.125
- weight_value: bfloat16 [2048, 2048], P(None, 'tp'), may hold values from -0.125 to 0.125
- bias_value: float32 [2048], P('tp'), may hold values from -3 to 3
- weight_out: bfloat16 [2048, 2048], P('tp'), may hold values from -2 to 2
- bias_out: float32 [2048], replicated, may hold values from -3 to 3
- weight_up: bfloat16 [2048, 8192], P(None, 'tp'), may hold values from -0.125 to 0.125
- bias_up: float32 [8192], P('tp'), may hold values from -3 to 3
- weight_down: bfloat16 [8192, 2048], P('tp'), may hold values from -0.0625 to 0.0625
- bias_down: float32 [2048], replicated, may hold values from -3 to 3
- gain_in: float32 [2048], replicated, may hold values from 0.25 to 1.75
- shift_in: float32 [2048], replicated, may hold values from -2 to 2
- gain_mid: float32 [2048], replicated, may hold values from 0.25 to 1.75
- shift_mid: float32 [2048], replicated, may hold values from -2 to 2
- cotangent: bfloat16 [16, 1024, 2048], P('dp', 'tp'), may hold values from -6 to 6
Outputs:
- output: bfloat16 [16, 1024, 2048], P('dp', 'tp')
- grad_tokens: float32 [16, 1024, 2048], P('dp', 'tp')
- grad_weight_query: float32 [2048, 2048], P('dp', 'tp')
- grad_bias_query: float32 [2048], P(('tp', 'dp'))
- grad_weight_key: float32 [2048, 2048], P('dp', 'tp')
- grad_weight_value: float32 [2048, 2048], P('dp', 'tp')
- grad_bias_value: float32 [2048], P(('tp', 'dp'))
- grad_weight_out: float32 [2048, 2048], P('tp', 'dp')
- grad_bias_out: float32 [2048], P('dp')
- grad_weight_up: float32 [2048, 8192], P('dp', 'tp')
- grad_bias_up: float32 [8192], P(('tp', 'dp'))
- grad_weight_down: float32 [8192, 2048], P('tp', 'dp')
- grad_bias_down: float32 [2048], P('dp')
- grad_gain_in: float32 [2048], P('dp')
- grad_shift_in: float32 [2048], P('dp')
- grad_gain_mid: float32 [2048], P('dp')
- grad_shift_mid: float32 [2048], P('dp')
Inputs may be any that keep to these rules, and one draw needn't show every extreme that they name: `lengths`: among the 2 sequences of one index of dp, one drawn from the seed has length 1024.
All inputs are finite; a program needn't handle non-finite values.
Results may differ from a plain program's by a relative error of at most 0.035.
Values may be sent and summed in bfloat16 or wider, within the bound.
No kernel may reach another device: no remote copies, remote signals or barrier semaphores. Data moves between devices by JAX's collectives and lax.ppermute only.
A program may use at most 192 MiB of HBM per device.

v0:
```python
import jax
import jax.numpy as jnp
from jax import lax
from jax.sharding import PartitionSpec as P

HEAD = 64
LAYER = 12
EPS = 1e-05
MASKED = -1e30
block_rows = 512


def sent_to_all(shard, axis):
    copies = jnp.broadcast_to(shard, (lax.axis_size(axis), *shard.shape))
    return lax.all_to_all(copies, axis, split_axis=0, concat_axis=0, tiled=True)


def over_copies(shard, axis):
    everything = sent_to_all(shard, axis)
    return jnp.sum(everything.astype(jnp.float32), axis=0)


def in_blocks(shard, dim, size):
    before, after = (shard.shape[:dim], shard.shape[dim + 1 :])
    return jnp.moveaxis(shard.reshape(*before, size, -1, *after), dim, 0)


def sum_packed(arrays, axis, dims):
    size = lax.axis_size(axis)
    pieces = [in_blocks(a, dim, size) for a, dim in zip(arrays, dims)]
    lines = jnp.concatenate([b.reshape(size, -1) for b in pieces], axis=1)
    width = max(16, -(-lines.shape[1] // 1024) * 8)
    lines = jnp.pad(lines, ((0, 0), (0, width * 128 - lines.shape[1]))).reshape(-1, 128)
    vector, at, outs = (lax.psum_scatter(lines, axis, tiled=True).reshape(-1), 0, [])
    for b in pieces:
        part = b[0]
        outs.append(vector[at : at + part.size].reshape(part.shape))
        at += part.size
    return tuple(outs)


def norm_rows(values, norm_gain, norm_bias):
    average = jnp.mean(values, -1, keepdims=True)
    centred = values - average
    variance = jnp.mean(centred * centred, -1, keepdims=True)
    inverse = lax.rsqrt(variance + EPS)
    normed = centred * inverse
    return (normed, inverse, normed * norm_gain + norm_bias)


def norm_back(upstream, normed, inverse, norm_gain):
    scaled = upstream * norm_gain
    mean_term = jnp.mean(scaled, -1, keepdims=True)
    proj_term = jnp.mean(scaled * normed, -1, keepdims=True)
    return inverse * (scaled - mean_term - normed * proj_term)


def masked_scores(query_block, key_vecs, offset, length):
    column_index = jnp.arange(key_vecs.shape[0])
    row_index = offset + jnp.arange(query_block.shape[0])
    allowed = (column_index[None, :] <= row_index[:, None]) & (column_index[None, :] < length)
    scores = jnp.einsum("qhd,khd->hqk", query_block, key_vecs, preferred_element_type=jnp.float32)
    return jnp.where(allowed[None], scores, MASKED)


def attend_forward(queries, key_vecs, value_vecs, length, block_len):
    outputs = []
    totals = []
    for offset in range(0, key_vecs.shape[0], block_len):
        query_block = queries[offset : offset + block_len]
        scores = masked_scores(query_block, key_vecs, offset, length)
        row_max = jnp.max(scores, -1, keepdims=True)
        exponent = jnp.exp(scores - row_max)
        row_sum = jnp.sum(exponent, -1, keepdims=True)
        soft_weights = (exponent / row_sum).astype(jnp.bfloat16)
        block_context = jnp.einsum(
            "hqk,khd->qhd", soft_weights, value_vecs, preferred_element_type=jnp.float32
        )
        outputs.append(block_context.astype(jnp.bfloat16))
        totals.append(row_max[..., 0] + jnp.log(row_sum[..., 0]))
    return (jnp.concatenate(outputs, 0), jnp.concatenate(totals, 1))


def attend_backward(queries, key_vecs, value_vecs, grad_context, length, log_total, block_len):
    key_grad = jnp.zeros(key_vecs.shape, jnp.float32)
    value_grad = jnp.zeros(value_vecs.shape, jnp.float32)
    query_grads = []
    for offset in range(0, key_vecs.shape[0], block_len):
        query_block = queries[offset : offset + block_len]
        grad_block = grad_context[offset : offset + block_len]
        scores = masked_scores(query_block, key_vecs, offset, length)
        soft_weights = jnp.exp(scores - log_total[:, offset : offset + block_len, None])
        value_grad = value_grad + jnp.einsum(
            "hqk,qhd->khd",
            soft_weights.astype(jnp.bfloat16),
            grad_block,
            preferred_element_type=jnp.float32,
        )
        grad_weights = jnp.einsum(
            "qhd,khd->hqk", grad_block, value_vecs, preferred_element_type=jnp.float32
        )
        weighted_sum = jnp.sum(soft_weights * grad_weights, -1, keepdims=True)
        grad_scores = (soft_weights * (grad_weights - weighted_sum)).astype(jnp.bfloat16)
        query_grads.append(
            jnp.einsum(
                "hqk,khd->qhd", grad_scores, key_vecs, preferred_element_type=jnp.float32
            ).astype(jnp.bfloat16)
        )
        key_grad = key_grad + jnp.einsum(
            "hqk,qhd->khd", grad_scores, query_block, preferred_element_type=jnp.float32
        )
    return (
        jnp.concatenate(query_grads, 0),
        key_grad.astype(jnp.bfloat16),
        value_grad.astype(jnp.bfloat16),
    )


def column_sum(values):
    return jnp.sum(values, (0, 1))


def on_device(
    tokens,
    lengths,
    exit_layers,
    weight_query,
    bias_query,
    weight_key,
    weight_value,
    bias_value,
    weight_out,
    bias_out,
    weight_up,
    bias_up,
    weight_down,
    bias_down,
    gain_in,
    shift_in,
    gain_mid,
    shift_mid,
    cotangent,
):
    tp_count = lax.axis_size("tp")
    tp_index = lax.axis_index("tp")
    seq_count, own_len, features = tokens.shape
    seq_len = own_len * tp_count
    row_count = seq_count * seq_len
    head_cols = weight_query.shape[1]
    heads_here = head_cols // HEAD
    block_len = min(block_rows, seq_len)
    query_scale = HEAD ** (-0.5)
    first_row = tp_index * own_len
    positions = jnp.arange(seq_len)
    live_full = ((positions[None, :] < lengths[:, None]) & (exit_layers >= LAYER)).astype(
        jnp.float32
    )[..., None]

    def split_heads(values):
        return values.reshape(seq_count, seq_len, heads_here, HEAD)

    live_own = lax.dynamic_slice_in_dim(live_full, first_row, own_len, 1)
    tokens_own = tokens.astype(jnp.float32)
    grad_own = cotangent.astype(jnp.float32)
    normed_in, inverse_in, normed_out = norm_rows(tokens_own, gain_in, shift_in)
    hidden_in = lax.all_gather(normed_out.astype(jnp.bfloat16), "tp", axis=1, tiled=True)
    in_matrix = hidden_in.reshape(row_count, features)
    weight_joined = jnp.concatenate((weight_query, weight_key, weight_value), 1)
    joined = jnp.dot(in_matrix, weight_joined, preferred_element_type=jnp.float32)
    queries = ((joined[:, :head_cols] + bias_query) * query_scale).astype(jnp.bfloat16)
    key_vecs = joined[:, head_cols : 2 * head_cols].astype(jnp.bfloat16)
    value_vecs = (joined[:, 2 * head_cols :] + bias_value).astype(jnp.bfloat16)
    context, log_total = lax.map(
        lambda packed: attend_forward(packed[0], packed[1], packed[2], packed[3], block_len),
        (split_heads(queries), split_heads(key_vecs), split_heads(value_vecs), lengths),
    )
    context_matrix = context.reshape(row_count, head_cols)
    partial_value = (
        jnp.dot(context_matrix, weight_out, preferred_element_type=jnp.float32)
        .astype(jnp.bfloat16)
        .reshape(seq_count, seq_len, features)
    )
    attention = lax.psum_scatter(partial_value, "tp", scatter_dimension=1, tiled=True).astype(
        jnp.float32
    )
    mid_own = tokens_own + live_own * (attention + bias_out)
    normed_mid, inverse_mid, mid_out = norm_rows(mid_own, gain_mid, shift_mid)
    hidden_mid = lax.all_gather(mid_out.astype(jnp.bfloat16), "tp", axis=1, tiled=True)
    mid_matrix = hidden_mid.reshape(row_count, features)
    up_sum = jnp.dot(mid_matrix, weight_up, preferred_element_type=jnp.float32) + bias_up
    activated = jax.nn.gelu(up_sum).astype(jnp.bfloat16)
    down_part = (
        jnp.dot(activated, weight_down, preferred_element_type=jnp.float32)
        .astype(jnp.bfloat16)
        .reshape(seq_count, seq_len, features)
    )
    branch = lax.psum_scatter(down_part, "tp", scatter_dimension=1, tiled=True).astype(jnp.float32)
    output = (mid_own + live_own * (branch + bias_down)).astype(jnp.bfloat16)
    grad_full = lax.all_gather(cotangent, "tp", axis=1, tiled=True)
    grad_live = (
        (grad_full.astype(jnp.float32) * live_full)
        .astype(jnp.bfloat16)
        .reshape(row_count, features)
    )
    grad_weight_down = jnp.einsum(
        "rf,rd->fd", activated, grad_live, preferred_element_type=jnp.float32
    )
    grad_activated = jnp.einsum(
        "rd,fd->rf", grad_live, weight_down, preferred_element_type=jnp.float32
    )
    grad_up_sum = jax.vjp(jax.nn.gelu, up_sum)[1](grad_activated)[0].astype(jnp.bfloat16)
    grad_bias_up = jnp.sum(grad_up_sum.astype(jnp.float32), 0)
    grad_weight_up = jnp.einsum(
        "rd,rf->df", mid_matrix, grad_up_sum, preferred_element_type=jnp.float32
    )
    mid_grad_part = jnp.einsum(
        "rf,df->rd", grad_up_sum, weight_up, preferred_element_type=jnp.float32
    ).reshape(seq_count, seq_len, features)
    mid_grad = lax.psum_scatter(
        mid_grad_part.astype(jnp.bfloat16), "tp", scatter_dimension=1, tiled=True
    ).astype(jnp.float32)
    back_own = grad_own + norm_back(mid_grad, normed_mid, inverse_mid, gain_mid)
    back_low = lax.all_gather((back_own * live_own).astype(jnp.bfloat16), "tp", axis=1, tiled=True)
    back_matrix = back_low.reshape(row_count, features)
    grad_weight_out = jnp.einsum(
        "rc,rd->cd", context_matrix, back_matrix, preferred_element_type=jnp.float32
    )
    grad_context = jnp.einsum(
        "rd,cd->rc", back_matrix, weight_out, preferred_element_type=jnp.float32
    ).astype(jnp.bfloat16)
    grad_queries, grad_keys, grad_values = lax.map(
        lambda packed: attend_backward(
            packed[0], packed[1], packed[2], packed[3], packed[4], packed[5], block_len
        ),
        (
            split_heads(queries),
            split_heads(key_vecs),
            split_heads(value_vecs),
            split_heads(grad_context),
            lengths,
            log_total,
        ),
    )
    grad_joined = jnp.concatenate(
        (
            grad_queries.reshape(row_count, head_cols) * query_scale,
            grad_keys.reshape(row_count, head_cols),
            grad_values.reshape(row_count, head_cols),
        ),
        1,
    )
    grad_weight_joined = jnp.einsum(
        "rd,rc->dc", in_matrix, grad_joined, preferred_element_type=jnp.float32
    )
    grad_bias_query = jnp.sum(grad_joined[:, :head_cols].astype(jnp.float32), 0)
    grad_bias_value = jnp.sum(grad_joined[:, 2 * head_cols :].astype(jnp.float32), 0)
    in_grad_part = jnp.einsum(
        "rc,dc->rd", grad_joined, weight_joined, preferred_element_type=jnp.float32
    ).reshape(seq_count, seq_len, features)
    in_grad = lax.psum_scatter(
        in_grad_part.astype(jnp.bfloat16), "tp", scatter_dimension=1, tiled=True
    ).astype(jnp.float32)
    grad_tokens = back_own + norm_back(in_grad, normed_in, inverse_in, gain_in)
    row_totals = (
        over_copies(column_sum(in_grad * normed_in).astype(jnp.bfloat16), "tp").astype(jnp.float32),
        over_copies(column_sum(in_grad).astype(jnp.bfloat16), "tp").astype(jnp.float32),
        over_copies(column_sum(mid_grad * normed_mid).astype(jnp.bfloat16), "tp").astype(
            jnp.float32
        ),
        over_copies(column_sum(mid_grad).astype(jnp.bfloat16), "tp").astype(jnp.float32),
        over_copies(column_sum(back_own * live_own).astype(jnp.bfloat16), "tp").astype(jnp.float32),
        over_copies(column_sum(grad_own * live_own).astype(jnp.bfloat16), "tp").astype(jnp.float32),
    )
    reduced = tuple(
        (
            part.astype(jnp.float32)
            for part in sum_packed(
                (
                    grad_weight_joined[:, :head_cols].astype(jnp.bfloat16),
                    grad_bias_query.astype(jnp.bfloat16),
                    grad_weight_joined[:, head_cols : 2 * head_cols].astype(jnp.bfloat16),
                    grad_weight_joined[:, 2 * head_cols :].astype(jnp.bfloat16),
                    grad_bias_value.astype(jnp.bfloat16),
                    grad_weight_out.astype(jnp.bfloat16),
                    row_totals[4].astype(jnp.bfloat16),
                    grad_weight_up.astype(jnp.bfloat16),
                    grad_bias_up.astype(jnp.bfloat16),
                    grad_weight_down.astype(jnp.bfloat16),
                    row_totals[5].astype(jnp.bfloat16),
                    row_totals[0].astype(jnp.bfloat16),
                    row_totals[1].astype(jnp.bfloat16),
                    row_totals[2].astype(jnp.bfloat16),
                    row_totals[3].astype(jnp.bfloat16),
                ),
                "dp",
                (0, 0, 0, 0, 0, 1, 0, 0, 0, 1, 0, 0, 0, 0, 0),
            )
        )
    )
    return (output, grad_tokens) + tuple(reduced)


def solution(mesh):
    return jax.shard_map(
        on_device,
        mesh=mesh,
        in_specs=(
            P("dp", "tp", None),
            P("dp"),
            P("dp", None),
            P(None, "tp"),
            P("tp"),
            P(None, "tp"),
            P(None, "tp"),
            P("tp"),
            P("tp", None),
            P(),
            P(None, "tp"),
            P("tp"),
            P("tp", None),
            P(),
            P(),
            P(),
            P(),
            P(),
            P("dp", "tp", None),
        ),
        out_specs=(
            P("dp", "tp", None),
            P("dp", "tp", None),
            P("dp", "tp"),
            P(("tp", "dp")),
            P("dp", "tp"),
            P("dp", "tp"),
            P(("tp", "dp")),
            P("tp", "dp"),
            P("dp"),
            P("dp", "tp"),
            P(("tp", "dp")),
            P("tp", "dp"),
            P("dp"),
            P("dp"),
            P("dp"),
            P("dp"),
            P("dp"),
        ),
        check_vma=False,
    )
```

profile of v0, /device:TPU:0, one launch (start us, length us, event | category | flops | bytes accessed | tf_op | source)
XLA Modules:
  0.0 950.4 jit_solution(8223075998611346334)
XLA Ops:
  17.6 50.0 %all-gather.5.cloned.1.call-done = bf16[2,1024,2048]{2,1,0:T(8,128)(2,1)} async-done(((bf16[2,64,2048]{2,1,0:T(8,128)(2,1)}), bf16[2,1024,2048]{2,1,0:T(8,128)(2,1)}) %all-gather.5.cloned.1.call-update) | async-done | bytes 8388624 | tf_op jit(solution)/shard_map/all_gather | solution.py:166
  67.6 7.4 fusion.130
  77.4 2.4 copy.77
  81.2 2.4 copy.78
  83.6 3.2 reshape.415
  86.8 3.5 copy.76
  91.2 19.9 %while.26 = (s32[]{:T(128)}, bf16[2,1024,2,64]{1,3,2,0:T(8,128)(2,1)}, f32[2,2,1024]{2,1,0:T(2,128)S(1)}, bf16[2,1024,2,64]{1,3,2,0:T(8,128)(2,1)}, s32[2]{0:T(1...) while((s32[]{:T(128)}, ...), condition=%wide.region_7.8_spmd, body=%wide.region_2.7_spmd.sunk | while | flops 558499328 | bytes 37839596 | solution.py:173
  113.0 6.8 convolution_convert_fusion.5
  121.0 95.0 %reduce-scatter.6.cloned.1.call-done = bf16[2,64,2048]{2,1,0:T(8,128)(2,1)} async-done(((bf16[2,1024,2048]{2,1,0:T(8,128)(2,1)}), bf16[2,64,2048]{2,1,0:T(8,128)(2,1)}) %reduce-scatter.6.cloned.1.call-update) | async-done | bytes 524304 | tf_op jit(solution)/shard_map/reduce_scatter | solution.py:183
  221.3 51.0 %all-gather.9.cloned.1.call-done = bf16[2,1024,2048]{2,1,0:T(8,128)(2,1)} async-done(((bf16[2,64,2048]{2,1,0:T(8,128)(2,1)}), bf16[2,1024,2048]{2,1,0:T(8,128)(2,1)}) %all-gather.9.cloned.1.call-update) | async-done | bytes 8388624 | tf_op jit(solution)/shard_map/all_gather | solution.py:199
  272.3 8.0 multiply_convert_fusion.2
  280.3 47.1 %all-gather.7.cloned.1.call-done = bf16[2,1024,2048]{2,1,0:T(8,128)(2,1)} async-done(((bf16[2,64,2048]{2,1,0:T(8,128)(2,1)}), bf16[2,1024,2048]{2,1,0:T(8,128)(2,1)}) %all-gather.7.cloned.1.call-update) | async-done | bytes 8388624 | tf_op jit(solution)/shard_map/all_gather | solution.py:188
  327.4 7.7 fusion.131
  335.1 8.4 fusion.126
  343.6 7.0 convolution_convert_fusion.3
  350.6 96.1 %reduce-scatter.10.cloned.1.call-done = bf16[2,64,2048]{2,1,0:T(8,128)(2,1)} async-done(((bf16[2,1024,2048]{2,1,0:T(8,128)(2,1)}), bf16[2,64,2048]{2,1,0:T(8,128)(2,1)}) %reduce-scatter.10.cloned.1.call-update) | async-done | bytes 524304 | tf_op jit(solution)/shard_map/reduce_scatter | solution.py:219
  448.5 2.9 multiply_convert_fusion.4
  451.9 54.2 %all-gather.11.cloned.1.call-done = bf16[2,1024,2048]{2,1,0:T(8,128)(2,1)} async-done(((bf16[2,64,2048]{2,1,0:T(8,128)(2,1)}), bf16[2,1024,2048]{2,1,0:T(8,128)(2,1)}) %all-gather.11.cloned.1.call-update) | async-done | bytes 8388624 | tf_op jit(solution)/shard_map/all_gather | solution.py:223
  506.1 6.6 convolution_convert_fusion.10
  512.7 3.2 reshape.414
  515.8 3.5 copy.83
  521.9 33.4 %while.27 = (s32[]{:T(128)}, bf16[2,1024,2,64]{1,3,2,0:T(8,128)(2,1)}, bf16[2,1024,2,64]{1,3,2,0:T(8,128)(2,1)}, bf16[2,1024,2,64]{1,3,2,0:T(8,128)(2,1)}, bf16[...) while((s32[]{:T(128)}, ...), condition=%wide.region_18.19_spmd, body=%wide.region_15.18_spmd.sunk | while | flops 1370619392 | bytes 92100536 | solution.py:231
  560.3 8.7 convolution_convert_fusion.2
  569.2 10.1 %convolution_convert_fusion.4 = bf16[2048,2048]{1,0:T(8,128)(2,1)} fusion(bf16[512,2048]{1,0:T(8,128)(2,1)S(1)} %copy-done, f32[2048,512]{1,0:T(8,128)} %copy-done.55, f32[512]{0:T(512)S(1)} %copy-done.54), kind=kOutput, calls=%fused_computation.117 | convolution fusion | flops 4309647360 | bytes 14682112 | tf_op jit(solution)/shard_map/dot_general | solution.py:193
  579.4 11.3 %convolution_convert_fusion.6 = bf16[512,2048]{1,0:T(8,128)(2,1)} fusion(bf16[2048,2048]{1,0:T(8,128)(2,1)} %bitcast.256, f32[2048,512]{1,0:T(8,128)} %copy-done.55, f32[512]{0:T(512)S(1)} %copy-done.54), kind=kOutput, calls=%fused_computation.129 | convolution fusion | flops 4306501632 | bytes 14682112 | tf_op jit(solution)/shard_map/rf,rd->fd/dot_general | solution.py:205
  594.0 5.1 all-to-all-start.5
  599.1 66.2 %reduce-scatter.12.cloned.1.call-done = bf16[2,64,2048]{2,1,0:T(8,128)(2,1)} async-done(((bf16[2,1024,2048]{2,1,0:T(8,128)(2,1)}), bf16[2,64,2048]{2,1,0:T(8,128)(2,1)}) %reduce-scatter.12.cloned.1.call-update) | async-done | bytes 524304 | tf_op jit(solution)/shard_map/reduce_scatter | solution.py:260
  665.4 3.7 fusion.116
  670.8 7.5 all-to-all-start.4
  678.4 10.3 %convolution_convert_fusion.7 = bf16[2048,512]{1,0:T(8,128)(2,1)} fusion(bf16[2048,2048]{1,0:T(8,128)(2,1)} %bitcast.276, bf16[2048,512]{1,0:T(8,128)(2,1)} %copy-done.56), kind=kOutput, calls=%fused_computation.130 | convolution fusion | flops 4296015872 | bytes 12582912 | tf_op jit(solution)/shard_map/rd,rf->df/dot_general | solution.py:213
  688.6 3.9 reshape_reshape.15
  692.5 3.7 copy.113
  700.6 6.2 all-to-all-start.3
  706.7 9.7 %convolution_convert_fusion.8 = bf16[2048,384]{1,0:T(8,128)(2,1)} fusion(bf16[2048,2048]{1,0:T(8,128)(2,1)} %bitcast.274, bf16[2048,384]{0,1:T(8,128)(2,1)} %copy-done.22), kind=kOutput, calls=%fused_computation.131 | convolution fusion | flops 3222011904 | bytes 11534336 | tf_op jit(solution)/shard_map/rd,rc->dc/dot_general | solution.py:252
  718.1 5.8 all-to-all-start
  723.9 2.6 fusion.129
  730.3 5.7 all-to-all-start.1
  742.2 5.3 all-to-all-start.2
  747.7 4.9 convolution_convert_fusion.9
  760.5 4.5 dynamic-update-slice.2
  765.0 4.4 dynamic-update-slice.3
  770.8 4.4 dynamic-update-slice.5
  778.6 12.4 %dynamic-update-slice.7 = bf16[8,394848]{1,0:T(8,128)(2,1)} dynamic-update-slice(bf16[8,394848]{1,0:T(8,128)(2,1)} %dynamic-update-slice.6, bf16[8,131072]{1,0:T(8,128)(2,1)} %reshape_reshape.15, s32[]{} %constant.109, s32[]{} %constant.116) | dynamic-update-slice | bytes 4194308
  792.4 12.1 %dynamic-update-slice.9 = bf16[8,394848]{1,0:T(8,128)(2,1)} dynamic-update-slice(bf16[8,394848]{1,0:T(8,128)(2,1)} %dynamic-update-slice.8, bf16[8,131072]{1,0:T(8,128)(2,1)} %bitcast.255, s32[]{} %constant.109, s32[]{} %constant.118) | dynamic-update-slice | bytes 4194308
  811.8 6.8 pad.4
  818.6 8.4 reshape.407
  827.8 4.0 fusion.110
  831.7 101.0 %reduce-scatter.14.cloned.1.call-done = bf16[3088,128]{1,0:T(8,128)(2,1)} async-done(((bf16[24704,128]{1,0:T(8,128)(2,1)}), bf16[3088,128]{1,0:T(8,128)(2,1)}) %reduce-scatter.14.cloned.1.call-update) | async-done | bytes 790544 | tf_op jit(solution)/shard_map/reduce_scatter | solution.py:34
  (331 shorter events, 140.0 us)
Async XLA Ops:
  7.2 327.9 %copy-start = (bf16[512,2048]{1,0:T(8,128)(2,1)S(1)}, bf16[512,2048]{1,0:T(8,128)(2,1)}, u32[]{:S(2)}) copy-start(bf16[512,2048]{1,0:T(8,128)(2,1)} %param.35) | copy-start | bytes 6291460
  7.2 9.5 copy-start.19
  7.2 60.4 %all-gather.5.cloned.1.call-start = ((), (), s32[]{:S(2)}) async-start(), calls=%async_computation.11 | async-start | bytes 8912896 | tf_op jit(solution)/shard_map/all_gather | solution.py:166
  12.8 203.2 %reduce-scatter.6.cloned.1.call-start = ((), (), s32[]{:S(2)}) async-start(), calls=%async_computation.12 | async-start | bytes 8912896 | tf_op jit(solution)/shard_map/reduce_scatter | solution.py:183
  67.6 7.4 copy-start.50
  67.6 7.4 copy-start.51
  77.4 13.8 %copy-start.52 = (s32[2]{0:T(128)S(1)}, s32[2]{0:T(128)}, u32[]{:S(2)}) copy-start(s32[2]{0:T(128)} %param.24) | copy-start | bytes 28
  111.1 8.7 copy-start.2
  113.0 6.8 copy-start.7
  119.8 96.2 %copy-start.1 = (bf16[2,64,2048]{2,1,0:T(8,128)(2,1)S(1)}, bf16[2,64,2048]{2,1,0:T(8,128)(2,1)}, u32[]{:S(2)}) copy-start(bf16[2,64,2048]{2,1,0:T(8,128)(2,1)} %param.23) | copy-start | bytes 1572868
  119.8 96.2 %copy-start.20 = (f32[2048]{0:T(1024)S(1)}, f32[2048]{0:T(1024)}, u32[]{:S(2)}) copy-start(f32[2048]{0:T(1024)} %param.32) | copy-start | bytes 24580
  119.8 99.1 %copy-start.21 = (f32[2048]{0:T(1024)S(1)}, f32[2048]{0:T(1024)}, u32[]{:S(2)}) copy-start(f32[2048]{0:T(1024)} %param.39) | copy-start | bytes 24580
  119.8 99.0 %copy-start.42 = (f32[2048]{0:T(1024)S(1)}, f32[2048]{0:T(1024)}, u32[]{:S(2)}) copy-start(f32[2048]{0:T(1024)} %param.40) | copy-start | bytes 24580
  119.9 152.4 %all-gather.9.cloned.1.call-start = ((), (), s32[]{:S(2)}) async-start(), calls=%async_computation.15 | async-start | bytes 8912896 | tf_op jit(solution)/shard_map/all_gather | solution.py:199
  120.6 206.8 %all-gather.7.cloned.1.call-start = ((), (), s32[]{:S(2)}) async-start(), calls=%async_computation.13 | async-start | bytes 8912896 | tf_op jit(solution)/shard_map/all_gather | solution.py:188
  121.0 544.3 %copy-start.25 = (f32[2,64]{1,0:T(2,128)}, f32[2,64]{1,0:T(2,128)S(1)}, u32[]{:S(2)}) copy-start(f32[2,64]{1,0:T(2,128)S(1)} %constant_dynamic-slice_fusion) | copy-start | bytes 1540
  217.4 447.9 %copy-start.27 = (f32[2,64]{1,0:T(2,128)}, f32[2,64]{1,0:T(2,128)S(1)}, u32[]{:S(2)}) copy-start(f32[2,64]{1,0:T(2,128)S(1)} %broadcast_multiply_fusion.5) | copy-start | bytes 1540
  218.9 446.4 %copy-start.29 = (f32[2,64]{1,0:T(2,128)}, f32[2,64]{1,0:T(2,128)S(1)}, u32[]{:S(2)}) copy-start(f32[2,64]{1,0:T(2,128)S(1)} %add_rsqrt_fusion) | copy-start | bytes 1540
  221.2 225.5 %reduce-scatter.10.cloned.1.call-start = ((), (), s32[]{:S(2)}) async-start(), calls=%async_computation.16 | async-start | bytes 8912896 | tf_op jit(solution)/shard_map/reduce_scatter | solution.py:219
  327.4 7.7 copy-start.8
  327.4 7.7 copy-start.54
  335.1 8.5 copy-start.55
  335.1 8.5 copy-start.53
  343.6 7.0 copy-start.56
  350.6 155.5 %all-gather.11.cloned.1.call-start = ((), (), s32[]{:S(2)}) async-start(), calls=%async_computation.17 | async-start | bytes 8912896 | tf_op jit(solution)/shard_map/all_gather | solution.py:223
  448.5 216.9 %copy-start.35 = (f32[2,64]{1,0:T(2,128)}, f32[2,64]{1,0:T(2,128)S(1)}, u32[]{:S(2)}) copy-start(f32[2,64]{1,0:T(2,128)S(1)} %get-tuple-element.269) | copy-start | bytes 1540
  448.5 216.9 %copy-start.37 = (f32[2,64]{1,0:T(2,128)}, f32[2,64]{1,0:T(2,128)S(1)}, u32[]{:S(2)}) copy-start(f32[2,64]{1,0:T(2,128)S(1)} %get-tuple-element.270) | copy-start | bytes 1540
  451.4 213.9 %reduce-scatter.12.cloned.1.call-start = ((), (), s32[]{:S(2)}) async-start(), calls=%async_computation.18 | async-start | bytes 8912896 | tf_op jit(solution)/shard_map/reduce_scatter | solution.py:260
  521.9 3.6 copy-start.3
  538.5 3.6 copy-start.3
  555.3 4.2 copy-start.12
  560.3 8.8 copy-start.22
  569.1 258.5 %reduce-scatter.8.cloned.1.call-start = ((), (), s32[]{:S(2)}) async-start(), calls=%async_computation.14 | async-start | bytes 8912896 | tf_op jit(solution)/shard_map/reduce_scatter | solution.py:197
  579.3 86.0 %copy-start.4 = (bf16[2,64,2048]{2,1,0:T(8,128)(2,1)S(1)}, bf16[2,64,2048]{2,1,0:T(8,128)(2,1)}, u32[]{:S(2)}) copy-start(bf16[2,64,2048]{2,1,0:T(8,128)(2,1)} %reduce-scatter.6.cloned.1.call-done) | copy-start | bytes 1572868
  579.3 86.0 %copy-start.23 = (f32[2048]{0:T(1024)S(1)}, f32[2048]{0:T(1024)}, u32[]{:S(2)}) copy-start(f32[2048]{0:T(1024)} %param.37) | copy-start | bytes 24580
  579.4 86.0 %copy-start.32 = (f32[2,64]{1,0:T(2,128)S(1)}, f32[2,64]{1,0:T(2,128)}, u32[]{:S(2)}) copy-start(f32[2,64]{1,0:T(2,128)} %copy-done.31) | copy-start | bytes 1540
  579.4 86.0 %copy-start.40 = (f32[2,64]{1,0:T(2,128)S(1)}, f32[2,64]{1,0:T(2,128)}, u32[]{:S(2)}) copy-start(f32[2,64]{1,0:T(2,128)} %copy-done.39) | copy-start | bytes 1540
  594.0 76.8 %all-to-all-start.5 = ((bf16[16,2,1024]{2,1,0:T(2,128)(2,1)}), bf16[16,2,1024]{2,1,0:T(2,128)(2,1)S(1)}, u32[]{:S(2)}, u32[]{:S(2)}) async-start(bf16[16,2,1024]{2,1,0:T(2,128)(2,1)} %reshape.428), calls=%async_computation.9 | async-start | bytes 131072 | tf_op jit(solution)/shard_map/all_to_all | solution.py:15
  670.8 29.7 %all-to-all-start.4 = ((bf16[16,2,1024]{2,1,0:T(2,128)(2,1)}), bf16[16,2,1024]{2,1,0:T(2,128)(2,1)S(1)}, u32[]{:S(2)}, u32[]{:S(2)}) async-start(bf16[16,2,1024]{2,1,0:T(2,128)(2,1)} %reshape.426), calls=%async_computation.8 | async-start | bytes 131072 | tf_op jit(solution)/shard_map/all_to_all | solution.py:15
  688.6 7.6 copy-start.49
  700.6 17.6 %all-to-all-start.3 = ((bf16[16,2,1024]{2,1,0:T(2,128)(2,1)}), bf16[16,2,1024]{2,1,0:T(2,128)(2,1)S(1)}, u32[]{:S(2)}, u32[]{:S(2)}) async-start(bf16[16,2,1024]{2,1,0:T(2,128)(2,1)} %reshape.424), calls=%async_computation.7 | async-start | bytes 131072 | tf_op jit(solution)/shard_map/all_to_all | solution.py:15
  718.1 12.2 %all-to-all-start = ((bf16[16,2,1024]{2,1,0:T(2,128)(2,1)}), bf16[16,2,1024]{2,1,0:T(2,128)(2,1)S(1)}, u32[]{:S(2)}, u32[]{:S(2)}) async-start(bf16[16,2,1024]{2,1,0:T(2,128)(2,1)} %reshape.418), calls=%async_computation.4 | async-start | bytes 131072 | tf_op jit(solution)/shard_map/all_to_all | solution.py:15
  730.3 11.9 %all-to-all-start.1 = ((bf16[16,2,1024]{2,1,0:T(2,128)(2,1)}), bf16[16,2,1024]{2,1,0:T(2,128)(2,1)S(1)}, u32[]{:S(2)}, u32[]{:S(2)}) async-start(bf16[16,2,1024]{2,1,0:T(2,128)(2,1)} %reshape.420), calls=%async_computation.5 | async-start | bytes 131072 | tf_op jit(solution)/shard_map/all_to_all | solution.py:15
  742.2 33.8 %all-to-all-start.2 = ((bf16[16,2,1024]{2,1,0:T(2,128)(2,1)}), bf16[16,2,1024]{2,1,0:T(2,128)(2,1)}, u32[]{:S(2)}, u32[]{:S(2)}) async-start(bf16[16,2,1024]{2,1,0:T(2,128)(2,1)} %reshape.422), calls=%async_computation.6 | async-start | bytes 131072 | tf_op jit(solution)/shard_map/all_to_all | solution.py:15
  747.6 7.1 copy-start.48
  747.6 185.1 %reduce-scatter.14.cloned.1.call-start = ((), (), s32[]{:S(2)}) async-start(), calls=%async_computation.19 | async-start | bytes 7114752 | tf_op jit(solution)/shard_map/reduce_scatter | solution.py:34
  775.3 15.7 %copy-start.45 = (bf16[8,64]{1,0:T(8,128)(2,1)S(1)}, bf16[8,64]{1,0:T(8,128)(2,1)}, u32[]{:S(2)}) copy-start(bf16[8,64]{1,0:T(8,128)(2,1)} %reshape.399) | copy-start | bytes 3076
  778.5 31.8 %copy-start.34 = (bf16[8,256]{1,0:T(8,128)(2,1)S(1)}, bf16[8,256]{1,0:T(8,128)(2,1)}, u32[]{:S(2)}) copy-start(bf16[8,256]{1,0:T(8,128)(2,1)} %reshape.406) | copy-start | bytes 12292
  (36 other events, 45.8 us)
Sparse Core Ops, SparseCore 0:
  12.9 54.6 all-gather.4
  120.0 96.0 reduce-scatter.5
  217.7 54.5 all-gather.8
  274.4 52.9 all-gather.6
  350.7 96.0 reduce-scatter.9
  451.5 54.4 all-gather.10
  569.2 96.0 reduce-scatter.11
  667.7 101.1 reduce-scatter.7
  827.2 105.4 reduce-scatter.13
where the time goes:
time: 963 us; the launch traced here: 950 us
  waiting for transfers between devices  562 us (58%)
  local copies, waits for them, and re-layouts  140 us (15%)
  matrix products  130 us (13%)
  other arithmetic  66.6 us (7%)
  starting transfers between devices  36.5 us (4%)
  between operations  14.8 us (2%)
    reduce_scatter x1, waiting for transfers between devices, sum_packed(): lax.psum_scatter(lines, axis, tiled=True).reshape(-1)  101 us
    reduce_scatter x1, waiting for transfers between devices, on_device(): lax.psum_scatter(mid_grad_part.astype(jnp.bfloat16), 'tp', scatter_dimens...  96.1 us
    reduce_scatter x1, waiting for transfers between devices, on_device(): lax.psum_scatter(partial_value, 'tp', scatter_dimension=1, tiled=True)  95 us
    unnamed x126, local copies, waits for them, and re-layouts  67.7 us
    reduce_scatter x1, waiting for transfers between devices, on_device(): lax.psum_scatter(in_grad_part.astype(jnp.bfloat16), 'tp', scatter_dimensi...  66.2 us
    all_gather x1, waiting for transfers between devices, on_device(): lax.all_gather((back_own * live_own).astype(jnp.bfloat16), 'tp', axis=1,...  54.2 us
    all_gather x1, waiting for transfers between devices, on_device(): grad_full = lax.all_gather(cotangent, 'tp', axis=1, tiled=True)  51 us
    all_gather x1, waiting for transfers between devices, on_device(): lax.all_gather(normed_out.astype(jnp.bfloat16), 'tp', axis=1, tiled=True)  50 us
  transfers between devices with their start and end apart: 15, of which 9 were waited for; matrix products, arithmetic and copies ran while one was open for 19% of the time, Pallas kernels for 0%

commit v1 on v0

--- a/solution.py
+++ b/solution.py
@@ -196,7 +196,9 @@
     )
     branch = lax.psum_scatter(down_part, "tp", scatter_dimension=1, tiled=True).astype(jnp.float32)
     output = (mid_own + live_own * (branch + bias_down)).astype(jnp.bfloat16)
-    grad_full = lax.all_gather(cotangent, "tp", axis=1, tiled=True)
+    grad_full = jnp.concatenate(
+        lax.all_to_all(jnp.stack([cotangent] * lax.axis_size("tp")), "tp", 0, 0), axis=1
+    )
     grad_live = (
         (grad_full.astype(jnp.float32) * live_full)
         .astype(jnp.bfloat16)

time: 963 us -> 1040 us (1.080)
  waiting for transfers between devices: 562 us -> 607 us
  starting transfers between devices: 36.5 us -> 53.5 us
  other arithmetic: 66.6 us -> 79.1 us
    all_to_all x0 -> x1, waiting for transfers between devices: none -> 153 us  [on_device(): lax.all_to_all(jnp.stack([cotangent] * lax.axis_size('tp')), 'tp', 0, 0)]
    all_gather x1 -> x0, waiting for transfers between devices: 51 us -> none  [on_device(): grad_full = lax.all_gather(cotangent, 'tp', axis=1, tiled=True)]
    all_gather x1, waiting for transfers between devices: 47.1 us -> 0.01 us  [on_device(): lax.all_gather(mid_out.astype(jnp.bfloat16), 'tp', axis=1, tiled=True)]
    reduce_scatter x1, waiting for transfers between devices: 96.1 us -> 84.8 us  [on_device(): lax.psum_scatter(mid_grad_part.astype(jnp.bfloat16), 'tp', scatter_dimens...]
    convert_element_type x0 -> x1, other arithmetic: none -> 11.2 us  [on_device(): grad_full.astype(jnp.float32) * live_full]
    all_gather x1, starting transfers between devices: 0.04 us -> 10.6 us  [on_device(): lax.all_gather((back_own * live_own).astype(jnp.bfloat16), 'tp', axis=1,...]
    unnamed x126 -> x127, local copies, waits for them, and re-layouts: 67.7 us -> 67.9 us
  transfers between devices with their start and end apart: 15 -> 15, of which waited for: 9 -> 8; matrix products, arithmetic and copies ran while one was open for 19% -> 18% of each run, Pallas kernels for 0% -> 0%
where the time goes in v1:
time: 1040 us; the launch traced here: 1030 us
  waiting for transfers between devices  607 us (58%)
  local copies, waits for them, and re-layouts  145 us (14%)
  matrix products  130 us (12%)
  other arithmetic  79.1 us (8%)
  starting transfers between devices  53.5 us (5%)
  between operations  15.3 us (1%)
    all_to_all x1, waiting for transfers between devices, on_device(): lax.all_to_all(jnp.stack([cotangent] * lax.axis_size('tp')), 'tp', 0, 0)  153 us
    reduce_scatter x1, waiting for transfers between devices, sum_packed(): lax.psum_scatter(lines, axis, tiled=True).reshape(-1)  101 us
    reduce_scatter x1, waiting for transfers between devices, on_device(): lax.psum_scatter(partial_value, 'tp', scatter_dimension=1, tiled=True)  95.4 us
    reduce_scatter x1, waiting for transfers between devices, on_device(): lax.psum_scatter(mid_grad_part.astype(jnp.bfloat16), 'tp', scatter_dimens...  84.8 us
    unnamed x127, local copies, waits for them, and re-layouts  67.9 us
    reduce_scatter x1, waiting for transfers between devices, on_device(): lax.psum_scatter(in_grad_part.astype(jnp.bfloat16), 'tp', scatter_dimensi...  66.1 us
    all_gather x1, waiting for transfers between devices, on_device(): lax.all_gather((back_own * live_own).astype(jnp.bfloat16), 'tp', axis=1,...  55.3 us
    all_gather x1, waiting for transfers between devices, on_device(): lax.all_gather(normed_out.astype(jnp.bfloat16), 'tp', axis=1, tiled=True)  50 us
  transfers between devices with their start and end apart: 15, of which 8 were waited for; matrix products, arithmetic and copies ran while one was open for 18% of the time, Pallas kernels for 0%

profile of v1, /device:TPU:0, one launch (start us, length us, event | category | flops | bytes accessed | tf_op | source)
XLA Modules:
  0.0 1031.1 jit_solution(16932344009959786705)
XLA Ops:
  17.6 50.0 %all-gather.4.cloned.1.call-done = bf16[2,1024,2048]{2,1,0:T(8,128)(2,1)} async-done(((bf16[2,64,2048]{2,1,0:T(8,128)(2,1)}), bf16[2,1024,2048]{2,1,0:T(8,128)(2,1)}) %all-gather.4.cloned.1.call-update) | async-done | bytes 8388624 | tf_op jit(solution)/shard_map/all_gather | solution.py:166
  67.6 7.4 fusion.131
  83.6 3.2 reshape.422
  86.8 3.5 copy.93
  91.1 19.9 %while.26 = (s32[]{:T(128)}, bf16[2,1024,2,64]{1,3,2,0:T(8,128)(2,1)}, f32[2,2,1024]{2,1,0:T(2,128)S(1)}, bf16[2,1024,2,64]{1,3,2,0:T(8,128)(2,1)}, s32[2]{0:T(1...) while((s32[]{:T(128)}, ...), condition=%wide.region_7.8_spmd, body=%wide.region_2.7_spmd.sunk | while | flops 558499328 | bytes 37839596 | solution.py:173
  112.9 6.8 convolution_convert_fusion.5
  120.6 95.4 %reduce-scatter.6.cloned.1.call-done = bf16[2,64,2048]{2,1,0:T(8,128)(2,1)} async-done(((bf16[2,1024,2048]{2,1,0:T(8,128)(2,1)}), bf16[2,64,2048]{2,1,0:T(8,128)(2,1)}) %reduce-scatter.6.cloned.1.call-update) | async-done | bytes 524304 | tf_op jit(solution)/shard_map/reduce_scatter | solution.py:183
  221.2 5.3 stack.2
  226.5 7.2 all-to-all-start
  233.9 153.2 %all-to-all-done = bf16[16,2,64,2048]{3,2,1,0:T(8,128)(2,1)} async-done(((bf16[16,2,64,2048]{3,2,1,0:T(8,128)(2,1)}), bf16[16,2,64,2048]{3,2,1,0:T(8,128)(2,1)}, u32[]{:S(2)}, u32[]{:S(2)}) %all-to-all-start) | async-done | bytes 8388640 | tf_op jit(solution)/shard_map/all_to_all | solution.py:200
  387.0 11.2 %copy_convert_fusion = f32[16,2,64,2048]{3,2,0,1:T(8,128)} fusion(bf16[16,2,64,2048]{3,2,1,0:T(8,128)(2,1)} %all-to-all-done), kind=kLoop, calls=%fused_computation.116 | loop fusion | flops 4194304 | bytes 25165824 | tf_op jit(solution)/shard_map/convert_element_type | solution.py:203
  398.3 9.2 fusion.89
  407.5 7.7 fusion.132
  415.2 8.4 fusion.127
  423.7 7.0 convolution_convert_fusion.3
  430.7 10.6 %all-gather.8.cloned.1.call-start = ((), (), s32[]{:S(2)}) async-start(), calls=%async_computation.17 | async-start | bytes 8912896 | tf_op jit(solution)/shard_map/all_gather | solution.py:225
  441.3 84.8 %reduce-scatter.10.cloned.1.call-done = bf16[2,64,2048]{2,1,0:T(8,128)(2,1)} async-done(((bf16[2,1024,2048]{2,1,0:T(8,128)(2,1)}), bf16[2,64,2048]{2,1,0:T(8,128)(2,1)}) %reduce-scatter.10.cloned.1.call-update) | async-done | bytes 524304 | tf_op jit(solution)/shard_map/reduce_scatter | solution.py:221
  527.7 2.9 multiply_convert_fusion.3
  530.7 55.3 %all-gather.8.cloned.1.call-done = bf16[2,1024,2048]{2,1,0:T(8,128)(2,1)} async-done(((bf16[2,64,2048]{2,1,0:T(8,128)(2,1)}), bf16[2,1024,2048]{2,1,0:T(8,128)(2,1)}) %all-gather.8.cloned.1.call-update) | async-done | bytes 8388624 | tf_op jit(solution)/shard_map/all_gather | solution.py:225
  586.1 6.6 convolution_convert_fusion.10
  592.6 3.2 reshape.421
  595.8 3.5 copy.101
  601.9 33.6 %while.27 = (s32[]{:T(128)}, bf16[2,1024,2,64]{1,3,2,0:T(8,128)(2,1)}, bf16[2,1024,2,64]{1,3,2,0:T(8,128)(2,1)}, bf16[2,1024,2,64]{1,3,2,0:T(8,128)(2,1)}, bf16[...) while((s32[]{:T(128)}, ...), condition=%wide.region_18.19_spmd, body=%wide.region_15.18_spmd.sunk | while | flops 1370619392 | bytes 92100536 | solution.py:233
  640.6 8.7 convolution_convert_fusion.2
  649.4 10.1 convolution_convert_fusion.4
  659.6 11.3 %convolution_convert_fusion.6 = bf16[512,2048]{1,0:T(8,128)(2,1)} fusion(bf16[2048,2048]{1,0:T(8,128)(2,1)} %fusion.89, f32[2048,512]{1,0:T(8,128)} %copy-done.55, f32[512]{0:T(512)S(1)} %copy-done.54), kind=kOutput, calls=%fused_computation.131 | convolution fusion | flops 4306501632 | bytes 14682112 | tf_op jit(solution)/shard_map/rf,rd->fd/dot_general | solution.py:207
  674.3 5.1 all-to-all-start.6
  679.4 66.1 %reduce-scatter.12.cloned.1.call-done = bf16[2,64,2048]{2,1,0:T(8,128)(2,1)} async-done(((bf16[2,1024,2048]{2,1,0:T(8,128)(2,1)}), bf16[2,64,2048]{2,1,0:T(8,128)(2,1)}) %reduce-scatter.12.cloned.1.call-update) | async-done | bytes 524304 | tf_op jit(solution)/shard_map/reduce_scatter | solution.py:262
  745.6 3.7 fusion.117
  751.0 7.5 all-to-all-start.5
  758.5 10.3 convolution_convert_fusion.7
  768.8 3.9 reshape_reshape.15
  772.7 3.6 copy.132
  780.7 5.9 all-to-all-start.4
  786.7 9.7 convolution_convert_fusion.8
  798.1 5.8 all-to-all-start.1
  810.3 5.7 all-to-all-start.2
  822.2 5.2 all-to-all-start.3
  827.6 4.9 convolution_convert_fusion.9
  840.4 4.4 dynamic-update-slice.2
  844.9 4.5 dynamic-update-slice.3
  850.7 4.4 dynamic-update-slice.5
  858.5 12.4 %dynamic-update-slice.7 = bf16[8,394848]{1,0:T(8,128)(2,1)} dynamic-update-slice(bf16[8,394848]{1,0:T(8,128)(2,1)} %dynamic-update-slice.6, bf16[8,131072]{1,0:T(8,128)(2,1)} %reshape_reshape.15, s32[]{} %constant.109, s32[]{} %constant.116) | dynamic-update-slice | bytes 4194308
  872.3 12.1 %dynamic-update-slice.9 = bf16[8,394848]{1,0:T(8,128)(2,1)} dynamic-update-slice(bf16[8,394848]{1,0:T(8,128)(2,1)} %dynamic-update-slice.8, bf16[8,131072]{1,0:T(8,128)(2,1)} %bitcast.265, s32[]{} %constant.109, s32[]{} %constant.118) | dynamic-update-slice | bytes 4194308
  891.7 6.8 pad.4
  898.5 8.4 reshape.413
  907.7 4.0 fusion.111
  911.6 101.1 %reduce-scatter.14.cloned.1.call-done = bf16[3088,128]{1,0:T(8,128)(2,1)} async-done(((bf16[24704,128]{1,0:T(8,128)(2,1)}), bf16[3088,128]{1,0:T(8,128)(2,1)}) %reduce-scatter.14.cloned.1.call-update) | async-done | bytes 790544 | tf_op jit(solution)/shard_map/reduce_scatter | solution.py:34
  (334 shorter events, 146.7 us)
Async XLA Ops:
  7.2 408.0 %copy-start = (bf16[512,2048]{1,0:T(8,128)(2,1)S(1)}, bf16[512,2048]{1,0:T(8,128)(2,1)}, u32[]{:S(2)}) copy-start(bf16[512,2048]{1,0:T(8,128)(2,1)} %param.35) | copy-start | bytes 6291460
  7.2 9.5 copy-start.19
  7.2 60.4 %all-gather.4.cloned.1.call-start = ((), (), s32[]{:S(2)}) async-start(), calls=%async_computation.12 | async-start | bytes 8912896 | tf_op jit(solution)/shard_map/all_gather | solution.py:166
  12.8 203.2 %reduce-scatter.6.cloned.1.call-start = ((), (), s32[]{:S(2)}) async-start(), calls=%async_computation.13 | async-start | bytes 8912896 | tf_op jit(solution)/shard_map/reduce_scatter | solution.py:183
  67.6 7.4 copy-start.51
  67.6 7.4 copy-start.52
  77.4 13.8 %copy-start.49 = (s32[2]{0:T(128)S(1)}, s32[2]{0:T(128)}, u32[]{:S(2)}) copy-start(s32[2]{0:T(128)} %param.24) | copy-start | bytes 28
  111.0 8.7 copy-start.2
  112.9 6.8 copy-start.7
  119.8 96.2 %copy-start.1 = (bf16[2,64,2048]{2,1,0:T(8,128)(2,1)S(1)}, bf16[2,64,2048]{2,1,0:T(8,128)(2,1)}, u32[]{:S(2)}) copy-start(bf16[2,64,2048]{2,1,0:T(8,128)(2,1)} %param.23) | copy-start | bytes 1572868
  119.8 96.2 %copy-start.20 = (f32[2048]{0:T(1024)S(1)}, f32[2048]{0:T(1024)}, u32[]{:S(2)}) copy-start(f32[2048]{0:T(1024)} %param.32) | copy-start | bytes 24580
  119.8 99.0 %copy-start.21 = (f32[2048]{0:T(1024)S(1)}, f32[2048]{0:T(1024)}, u32[]{:S(2)}) copy-start(f32[2048]{0:T(1024)} %param.39) | copy-start | bytes 24580
  119.8 99.0 %copy-start.43 = (f32[2048]{0:T(1024)S(1)}, f32[2048]{0:T(1024)}, u32[]{:S(2)}) copy-start(f32[2048]{0:T(1024)} %param.40) | copy-start | bytes 24580
  119.9 287.6 %all-gather.6.cloned.1.call-start = ((), (), s32[]{:S(2)}) async-start(), calls=%async_computation.14 | async-start | bytes 8912896 | tf_op jit(solution)/shard_map/all_gather | solution.py:188
  120.6 624.9 %copy-start.25 = (f32[2,64]{1,0:T(2,128)}, f32[2,64]{1,0:T(2,128)S(1)}, u32[]{:S(2)}) copy-start(f32[2,64]{1,0:T(2,128)S(1)} %constant_dynamic-slice_fusion) | copy-start | bytes 1540
  217.4 528.1 %copy-start.27 = (f32[2,64]{1,0:T(2,128)}, f32[2,64]{1,0:T(2,128)S(1)}, u32[]{:S(2)}) copy-start(f32[2,64]{1,0:T(2,128)S(1)} %broadcast_multiply_fusion.5) | copy-start | bytes 1540
  218.8 526.7 %copy-start.29 = (f32[2,64]{1,0:T(2,128)}, f32[2,64]{1,0:T(2,128)S(1)}, u32[]{:S(2)}) copy-start(f32[2,64]{1,0:T(2,128)S(1)} %add_rsqrt_fusion) | copy-start | bytes 1540
  226.5 160.5 %all-to-all-start = ((bf16[16,2,64,2048]{3,2,1,0:T(8,128)(2,1)}), bf16[16,2,64,2048]{3,2,1,0:T(8,128)(2,1)}, u32[]{:S(2)}, u32[]{:S(2)}) async-start(bf16[16,2,64,2048]{3,2,1,0:T(8,128)(2,1)} %stack.2), calls=%async_computation.2 | async-start | bytes 16777216 | tf_op jit(solution)/shard_map/all_to_all | solution.py:200
  233.7 292.3 %reduce-scatter.10.cloned.1.call-start = ((), (), s32[]{:S(2)}) async-start(), calls=%async_computation.16 | async-start | bytes 8912896 | tf_op jit(solution)/shard_map/reduce_scatter | solution.py:221
  407.5 7.7 copy-start.8
  407.5 7.7 copy-start.54
  415.2 8.5 copy-start.55
  415.2 8.5 copy-start.53
  423.7 7.0 copy-start.56
  430.7 155.4 %all-gather.8.cloned.1.call-start = ((), (), s32[]{:S(2)}) async-start(), calls=%async_computation.17 | async-start | bytes 8912896 | tf_op jit(solution)/shard_map/all_gather | solution.py:225
  527.7 217.8 %copy-start.36 = (f32[2,64]{1,0:T(2,128)}, f32[2,64]{1,0:T(2,128)S(1)}, u32[]{:S(2)}) copy-start(f32[2,64]{1,0:T(2,128)S(1)} %get-tuple-element.286) | copy-start | bytes 1540
  527.7 217.8 %copy-start.38 = (f32[2,64]{1,0:T(2,128)}, f32[2,64]{1,0:T(2,128)S(1)}, u32[]{:S(2)}) copy-start(f32[2,64]{1,0:T(2,128)S(1)} %get-tuple-element.287) | copy-start | bytes 1540
  530.7 214.8 %reduce-scatter.12.cloned.1.call-start = ((), (), s32[]{:S(2)}) async-start(), calls=%async_computation.18 | async-start | bytes 8912896 | tf_op jit(solution)/shard_map/reduce_scatter | solution.py:262
  601.9 3.6 copy-start.3
  618.5 3.6 copy-start.3
  635.5 4.2 copy-start.12
  640.6 8.8 copy-start.22
  649.3 258.2 %reduce-scatter.8.cloned.1.call-start = ((), (), s32[]{:S(2)}) async-start(), calls=%async_computation.15 | async-start | bytes 8912896 | tf_op jit(solution)/shard_map/reduce_scatter | solution.py:197
  659.6 86.0 %copy-start.4 = (bf16[2,64,2048]{2,1,0:T(8,128)(2,1)S(1)}, bf16[2,64,2048]{2,1,0:T(8,128)(2,1)}, u32[]{:S(2)}) copy-start(bf16[2,64,2048]{2,1,0:T(8,128)(2,1)} %reduce-scatter.6.cloned.1.call-done) | copy-start | bytes 1572868
  659.6 86.0 %copy-start.23 = (f32[2048]{0:T(1024)S(1)}, f32[2048]{0:T(1024)}, u32[]{:S(2)}) copy-start(f32[2048]{0:T(1024)} %param.37) | copy-start | bytes 24580
  659.6 86.0 %copy-start.33 = (f32[2,64]{1,0:T(2,128)S(1)}, f32[2,64]{1,0:T(2,128)}, u32[]{:S(2)}) copy-start(f32[2,64]{1,0:T(2,128)} %copy-done.32) | copy-start | bytes 1540
  659.6 86.0 %copy-start.41 = (f32[2,64]{1,0:T(2,128)S(1)}, f32[2,64]{1,0:T(2,128)}, u32[]{:S(2)}) copy-start(f32[2,64]{1,0:T(2,128)} %copy-done.40) | copy-start | bytes 1540
  674.3 76.7 %all-to-all-start.6 = ((bf16[16,2,1024]{2,1,0:T(2,128)(2,1)}), bf16[16,2,1024]{2,1,0:T(2,128)(2,1)S(1)}, u32[]{:S(2)}, u32[]{:S(2)}) async-start(bf16[16,2,1024]{2,1,0:T(2,128)(2,1)} %reshape.435), calls=%async_computation.10 | async-start | bytes 131072 | tf_op jit(solution)/shard_map/all_to_all | solution.py:15
  751.0 29.7 %all-to-all-start.5 = ((bf16[16,2,1024]{2,1,0:T(2,128)(2,1)}), bf16[16,2,1024]{2,1,0:T(2,128)(2,1)S(1)}, u32[]{:S(2)}, u32[]{:S(2)}) async-start(bf16[16,2,1024]{2,1,0:T(2,128)(2,1)} %reshape.433), calls=%async_computation.9 | async-start | bytes 131072 | tf_op jit(solution)/shard_map/all_to_all | solution.py:15
  768.8 7.6 copy-start.50
  780.7 17.4 %all-to-all-start.4 = ((bf16[16,2,1024]{2,1,0:T(2,128)(2,1)}), bf16[16,2,1024]{2,1,0:T(2,128)(2,1)S(1)}, u32[]{:S(2)}, u32[]{:S(2)}) async-start(bf16[16,2,1024]{2,1,0:T(2,128)(2,1)} %reshape.431), calls=%async_computation.8 | async-start | bytes 131072 | tf_op jit(solution)/shard_map/all_to_all | solution.py:15
  798.1 12.1 %all-to-all-start.1 = ((bf16[16,2,1024]{2,1,0:T(2,128)(2,1)}), bf16[16,2,1024]{2,1,0:T(2,128)(2,1)S(1)}, u32[]{:S(2)}, u32[]{:S(2)}) async-start(bf16[16,2,1024]{2,1,0:T(2,128)(2,1)} %reshape.425), calls=%async_computation.5 | async-start | bytes 131072 | tf_op jit(solution)/shard_map/all_to_all | solution.py:15
  810.3 12.0 %all-to-all-start.2 = ((bf16[16,2,1024]{2,1,0:T(2,128)(2,1)}), bf16[16,2,1024]{2,1,0:T(2,128)(2,1)S(1)}, u32[]{:S(2)}, u32[]{:S(2)}) async-start(bf16[16,2,1024]{2,1,0:T(2,128)(2,1)} %reshape.427), calls=%async_computation.6 | async-start | bytes 131072 | tf_op jit(solution)/shard_map/all_to_all | solution.py:15
  822.2 33.8 %all-to-all-start.3 = ((bf16[16,2,1024]{2,1,0:T(2,128)(2,1)}), bf16[16,2,1024]{2,1,0:T(2,128)(2,1)}, u32[]{:S(2)}, u32[]{:S(2)}) async-start(bf16[16,2,1024]{2,1,0:T(2,128)(2,1)} %reshape.429), calls=%async_computation.7 | async-start | bytes 131072 | tf_op jit(solution)/shard_map/all_to_all | solution.py:15
  827.5 7.1 copy-start.48
  827.5 185.2 %reduce-scatter.14.cloned.1.call-start = ((), (), s32[]{:S(2)}) async-start(), calls=%async_computation.19 | async-start | bytes 7114752 | tf_op jit(solution)/shard_map/reduce_scatter | solution.py:34
  855.2 15.7 %copy-start.45 = (bf16[8,64]{1,0:T(8,128)(2,1)S(1)}, bf16[8,64]{1,0:T(8,128)(2,1)}, u32[]{:S(2)}) copy-start(bf16[8,64]{1,0:T(8,128)(2,1)} %reshape.405) | copy-start | bytes 3076
  858.5 31.7 %copy-start.35 = (bf16[8,256]{1,0:T(8,128)(2,1)S(1)}, bf16[8,256]{1,0:T(8,128)(2,1)}, u32[]{:S(2)}) copy-start(bf16[8,256]{1,0:T(8,128)(2,1)} %reshape.412) | copy-start | bytes 12292
  (36 other events, 45.5 us)
Sparse Core Ops, SparseCore 0:
  12.9 54.6 all-gather.3
  120.0 95.9 reduce-scatter.5
  221.3 159.1 all-gather.5
  430.8 95.1 reduce-scatter.9
  530.8 55.2 all-gather.7
  649.5 96.0 reduce-scatter.11
  747.9 101.0 reduce-scatter.7
  907.1 105.5 reduce-scatter.13
